TPU v7x, 128 devices: a whole 4x4x4 slice. The times are simulated.
128 devices in a mesh: grp: 32 (over x, y, core), blk: 4 (over z).
Axes of the slice: x: 4, y: 4, z: 4, core: 2. Of those that a mesh axis runs over, the one named last changes fastest.
Arguments:
- embeddings: bfloat16 [65536, 1024], P(('grp', 'blk'))
- cluster_ids: int32 [65536, 1], P(('grp', 'blk')), may hold values from 0 to 31; in each aligned block of 512 rows (0 to 511, 512 to 1023, ...) at most 64 rows name the same one
- priority: int32 [65536], P(('grp', 'blk')), may hold values from 0 to 65535, each once
Outputs:
- best_match: float32 [65536], P(('grp', 'blk'))
Inputs may be any that keep to these rules, and one draw needn't show every extreme that they name: `cluster_ids`: the 512 rows of one device name one cluster at most 64 times, a bound that some block reaches.
All inputs are finite; a program needn't handle non-finite values.
Results may differ from a plain program's by a relative error of at most 0.00049.
Values may be sent and summed in bfloat16 or wider, within the bound.
A program may use at most 128 MiB of HBM per device.

v0:
```python
import jax
import jax.numpy as jnp
from jax import lax
from jax.sharding import PartitionSpec as P

SLOT = 64


never_rank = 2**30


def local(embeddings, cluster_ids, priority):
    width = embeddings.shape[1]
    groups = lax.axis_size("grp")
    slots = SLOT
    wide = embeddings.astype(jnp.float32)
    unit = (wide / jnp.sqrt(jnp.sum(wide * wide, axis=1, keepdims=True) + 1e-06)).astype(
        jnp.bfloat16
    )
    labels = cluster_ids[:, 0]
    onehot = (labels[:, None] == jnp.arange(groups, dtype=jnp.int32)[None, :]).astype(jnp.int32)
    before = jnp.cumsum(onehot, axis=0) - onehot
    position = jnp.sum(onehot * before, axis=1)
    target = labels * slots + position
    outbox = jnp.zeros((groups * slots, width), jnp.bfloat16).at[target].set(unit)
    outrank = jnp.full((groups * slots,), never_rank, jnp.int32).at[target].set(priority)
    inbox, inrank = (
        lax.all_to_all(
            outbox.reshape(groups, slots, width), "grp", split_axis=0, concat_axis=0, tiled=True
        ),
        lax.all_to_all(
            outrank.reshape(groups, slots), "grp", split_axis=0, concat_axis=0, tiled=True
        ),
    )
    query = inbox.reshape(groups * slots, width)
    q_rank = inrank.reshape(groups * slots)
    local_rows = groups * slots
    start_best = jnp.full((local_rows,), -1.0, jnp.float32)
    scores = lax.dot_general(
        query,
        lax.all_gather(query, "blk", axis=0, tiled=True),
        (((1,), (1,)), ((), ())),
        preferred_element_type=jnp.float32,
    )
    allowed = lax.all_gather(q_rank, "blk", axis=0, tiled=True)[None, :] < q_rank[:, None]
    best_local = jnp.maximum(
        start_best, jnp.max(jnp.where(allowed, scores, jnp.float32(-1.0)), axis=1)
    )
    returned = lax.all_to_all(
        best_local.reshape(groups, slots), "grp", split_axis=0, concat_axis=0, tiled=True
    )
    return returned.reshape(groups * slots)[target]


def solution(mesh):
    placed = (P(("grp", "blk"), None), P(("grp", "blk"), None), P(("grp", "blk")))
    return jax.shard_map(
        local, mesh=mesh, in_specs=placed, out_specs=P(("grp", "blk")), check_vma=False
    )
```

profile of v0, /device:TPU:1, one launch (start us, length us, event | category | flops | bytes accessed | tf_op | source)
XLA Modules:
  0.0 297.9 jit_solution(7682525953630342940)
XLA Ops:
  6.5 0.0 all-gather.2.cloned.1.call-start
  6.5 0.7 fusion.9
  7.2 1.2 reduce-window.6
  8.4 0.2 slice_reduce_fusion
  8.6 0.8 fusion.8
  9.4 0.7 compare_select_fusion
  10.1 1.5 fusion
  11.6 6.0 %scatter_custom_fusion.1 = bf16[2048,1024]{1,0:T(8,128)(2,1)} fusion(s32[512]{0:T(512)S(1)} %bitcast.32, bf16[]{:T(256)} %constant.4.clone.1, bf16[512,1024]{1,0:T(8,128)(2,1)} %param.3, f32[512]{0:T(512)S(1)} %add_sqrt_fusion), kind=kCustom, calls=%fused_computation.8 | custom fusion | flops 1572864 | bytes 5244930 | tf_op jit(solution)/shard_map/scatter | solution.py:25
  17.6 59.3 %all_to_all.20 = bf16[32,64,1024]{2,1,0:T(8,128)(2,1)} all-to-all(bf16[32,64,1024]{2,1,0:T(8,128)(2,1)} %bitcast.27), channel_id=1, replica_groups=mesh['grp'=32,'blk'=4] {'grp'}, dimensions={0} | all-to-all | bytes 8388608 | tf_op jit(solution)/shard_map/all_to_all | solution.py:28
  76.9 0.0 all-gather.2.cloned.1.call-update
  76.9 2.6 scatter_custom_fusion
  79.5 0.1 all_to_all.13
  79.6 10.7 %all_to_all.21 = s32[32,1,64]{2,1,0:T(1,128)S(1)} all-to-all(s32[32,1,64]{2,1,0:T(1,128)S(1)} %all_to_all.13), channel_id=1, replica_groups=mesh['grp'=32,'blk'=4] {'grp'}, dimensions={0} | all-to-all | bytes 16384 | tf_op jit(solution)/shard_map/all_to_all | solution.py:31
  90.3 0.5 broadcast.58
  90.8 0.7 reduce.8
  91.5 0.1 reshape.61
  91.6 11.5 %all_gather.6 = s32[8192]{0:T(1024)S(1)} all-gather(s32[2048]{0:T(1024)S(1)} %reshape.61), channel_id=1, replica_groups=mesh['grp'=32,'blk'=4] {'blk'}, dimensions={0}, use_global_device_ids=true | all-gather | bytes 40960 | tf_op jit(solution)/shard_map/all_gather | solution.py:45
  103.1 127.0 %all-gather.2.cloned.1.call-done = bf16[8192,1024]{1,0:T(8,128)(2,1)} async-done(((bf16[2048,1024]{1,0:T(8,128)(2,1)}), bf16[8192,1024]{1,0:T(8,128)(2,1)}) %all-gather.2.cloned.1.call-update) | async-done | bytes 16777232 | tf_op jit(solution)/shard_map/all_gather | solution.py:41
  230.1 40.3 %select_reduce_fusion = f32[2048]{0:T(1024)S(1)} fusion(bf16[2048,1024]{1,0:T(8,128)(2,1)} %bitcast.29, bf16[8192,1024]{1,0:T(8,128)(2,1)} %all-gather.2.cloned.1.call-done, s32[8192]{0:T(1024)S(1)} %all_gather.6, s32[2048]{0:T(1024)S(1)} %reshape.61), kind=kOutput, calls=%fused_computation.3 | convolution fusion | flops 34410070016 | bytes 21020672 | tf_op jit(solution)/shard_map/dot_general | solution.py:39
  270.4 0.7 max_broadcast_in_dim.15
  271.1 7.5 %all-to-all-start.2 = ((f32[32,1,64]{2,1,0:T(1,128)}), f32[32,1,64]{2,1,0:T(1,128)S(1)}, u32[]{:S(2)}, u32[]{:S(2)}) async-start(f32[32,1,64]{2,1,0:T(1,128)} %max_broadcast_in_dim.15), calls=%async_computation.2 | async-start | bytes 32768 | tf_op jit(solution)/shard_map/all_to_all | solution.py:49
  278.5 6.9 %all-to-all-done.2 = f32[32,1,64]{2,1,0:T(1,128)S(1)} async-done(((f32[32,1,64]{2,1,0:T(1,128)}), f32[32,1,64]{2,1,0:T(1,128)S(1)}, u32[]{:S(2)}, u32[]{:S(2)}) %all-to-all-start.2) | async-done | bytes 8224 | tf_op jit(solution)/shard_map/all_to_all | solution.py:49
  285.5 0.5 broadcast.59
  286.0 0.7 reduce.9
  286.7 0.1 reshape.64
  286.7 4.3 %gather_fusion = f32[512]{0:T(512)} fusion(f32[2048]{0:T(1024)S(1)} %reshape.64, s32[1024]{0:T(1024)S(1)} %pad_clamp_fusion), kind=kCustom, calls=%fused_computation | custom fusion | bytes 6144 | tf_op jit(solution)/shard_map/gather | solution.py:52
  (5 shorter events, 0.1 us)
Async XLA Ops:
  6.5 223.5 %all-gather.2.cloned.1.call-start = ((), (), s32[]{:S(2)}) async-start(), calls=%async_computation.3 | async-start | bytes 20971520 | tf_op jit(solution)/shard_map/all_gather | solution.py:41
  271.1 14.4 %all-to-all-start.2 = ((f32[32,1,64]{2,1,0:T(1,128)}), f32[32,1,64]{2,1,0:T(1,128)S(1)}, u32[]{:S(2)}, u32[]{:S(2)}) async-start(f32[32,1,64]{2,1,0:T(1,128)} %max_broadcast_in_dim.15), calls=%async_computation.2 | async-start | bytes 32768 | tf_op jit(solution)/shard_map/all_to_all | solution.py:49
Sparse Core Ops, SparseCore 0:
  77.1 152.9 all-gather.1
where the time goes:
time: 298 us
  waiting for transfers between devices  134 us (45%)
  blocking collectives  81.5 us (27%)
  matrix products  40.3 us (14%)
  between operations  13.5 us (5%)
  other arithmetic  12.2 us (4%)
  local copies, waits for them, and re-layouts  9.02 us (3%)
  starting transfers between devices  7.45 us (2%)
    all_gather x1, waiting for transfers between devices, local(): lax.all_gather(query, 'blk', axis=0, tiled=True)  127 us
    all_to_all x1, blocking collectives, local(): lax.all_to_all(outbox.reshape(groups, slots, width), 'grp', split_axis=0,...  59.3 us
    dot_general x1, matrix products, local(): lax.dot_general(query, lax.all_gather(query, 'blk', axis=0, tiled=True),...  40.3 us
    all_gather x1, blocking collectives, local(): lax.all_gather(q_rank, 'blk', axis=0, tiled=True)[None, :] < q_rank[:, None]  11.5 us
    all_to_all x1, blocking collectives, local(): lax.all_to_all(outrank.reshape(groups, slots), 'grp', split_axis=0, conca...  10.7 us
    all_to_all x1, starting transfers between devices, local(): lax.all_to_all(best_local.reshape(groups, slots), 'grp', split_axis=0, co...  7.45 us
    all_to_all x1, waiting for transfers between devices, local(): lax.all_to_all(best_local.reshape(groups, slots), 'grp', split_axis=0, co...  6.93 us
  transfers between devices with their start and end apart: 2, of which 2 were waited for; matrix products, arithmetic and copies ran while one was open for 1% of the time, Pallas kernels for 0%

commit v1 on v0

v1 whole, which is shorter than its diff:
```python
import functools

import jax
import jax.numpy as jnp
from jax import lax
from jax.experimental import pallas as pl
from jax.experimental.pallas import tpu as pltpu
from jax.sharding import PartitionSpec as P

MESH = pl.DeviceIdType.MESH
SIDE = 4
CHUNKS = 4
WIDTH = 1024
ROWS = 512
PART = ROWS // CHUNKS
CHIP = 2 * ROWS
STEP = ((1, 0, 0), (-1, 0, 0), (0, 1, 0), (0, -1, 0), (0, 0, 1), (0, 0, -1))

TREE = (
    (0, -1, -1, 0),
    (3, 0, 5, 1),
    (51, 1, 1, 1),
    (4, 0, 2, 1),
    (5, 3, 4, 1),
    (20, 3, 0, 1),
    (12, 0, 3, 1),
    (1, 0, 4, 2),
    (35, 2, 1, 2),
    (23, 5, 5, 2),
    (63, 2, 3, 2),
    (9, 4, 2, 2),
)
SLOTS = len(TREE)
OFFSET = [(v // 16, v // 4 % 4, v % 4) for v, _, _, _ in TREE]

BLOCK_US = 23.0
HOP_US = 0.7
UNIT_US = 1.43
SIBLING_US = 1.5


def difference(p, q):
    return tuple((a - b) % SIDE for a, b in zip(OFFSET[p], OFFSET[q]))


def arrivals():
    start = [0.0] * SLOTS
    for _ in range(SLOTS):
        for n in range(1, SLOTS):
            _, parent, way, wave = TREE[n]
            begin = 0.0 if parent == 0 else start[parent] + BLOCK_US / CHUNKS + HOP_US
            if wave == 2:
                for m in range(1, SLOTS):
                    if TREE[m][2] == way and TREE[m][3] == 1:
                        begin = max(begin, start[m] + BLOCK_US)
            start[n] = begin
    return [
        [0.0 if n == 0 else start[n] + HOP_US + BLOCK_US * (r + 1) / CHUNKS for r in range(CHUNKS)]
        for n in range(SLOTS)
    ]


def make_jobs(ready):
    best = {}
    for s in range(SLOTS):
        for t in range(SLOTS):
            if s == t:
                continue
            d, e = difference(s, t), difference(t, s)
            key = min(d, e)
            if d == e:
                axis = [k for k in range(3) if d[k] == 2][0] + 1
                when = max(ready[s][-1], ready[t][-1])
                jobs = [(when, s, t, 0, axis)]
                cost = 2 * when**3
            else:
                jobs = [
                    (max(ready[s][-1], ready[t][CHUNKS // 2 * (h + 1) - 1]), s, t, h, 0)
                    for h in range(2)
                ]
                cost = sum(j[0] ** 3 for j in jobs)
            if key not in best or cost < best[key][0]:
                best[key] = (cost, jobs)
    assert len(best) == SIDE**3 // 2 + 3
    return sorted(job for _, jobs in best.values() for job in jobs)


def plan():
    ready = arrivals()
    jobs = make_jobs(ready)
    events = sorted((ready[n][r], n, r) for n in range(1, SLOTS) for r in range(CHUNKS))
    steps = []
    seen = set()
    now = 0.0
    first = [[(0.0, 0, 0, 0, 0)] * 2, [(0.0, 0, 0, 1, 0)] * 2]
    queue = list(jobs)
    while queue or first:
        if first:
            mine, first = first, None
        else:
            take = queue[:4]
            queue = queue[4:]
            while len(take) < 4:
                take.append(take[-1])
            mine = [take[0::2], take[1::2]]
        now = max([now] + [j[0] + SIBLING_US for pair in mine for j in pair if j[0] > 0])
        arrived = []
        while events and events[0][0] <= now:
            arrived.append(events.pop(0)[1:])
        steps.append((arrived, mine))
        now += 2 * UNIT_US
    return steps, [e[1:] for e in events]


def kernel(steps, left, x_ref, cluster_ref, rank_ref, out_ref, rows, keys, columns, row_best, col_best, outbox,
           inbox, send, arrive, send_sib, arrive_sib, key_send, key_arrive, key_send_sib, key_arrive_sib,
           back_send, back_arrive):
    grp, z = lax.axis_index("grp"), lax.axis_index("blk")
    x, y, core = grp // (2 * SIDE), grp // 2 % SIDE, grp % 2
    other = 1 - core

    def device(offset, which):
        dx, dy, dz = offset
        return (
            (x + dx + SIDE) % SIDE * (2 * SIDE) + (y + dy + SIDE) % SIDE * 2 + which,
            (z + dz + SIDE) % SIDE,
        )

    neighbours = [device(step, core) for step in STEP]
    sibling = device((0, 0, 0), other)
    children = {n: [m for m in range(1, SLOTS) if TREE[m][1] == n] for n in range(SLOTS)}

    def part(n, r, which):
        return rows.at[n, pl.ds(pl.multiple_of(r * 2 * PART + which * PART, PART), PART)]

    def hop(n, r):
        way = TREE[n][2] ^ 1
        return pltpu.make_async_remote_copy(
            src_ref=part(TREE[n][1], r, core), dst_ref=part(n, r, core), send_sem=send.at[n, r],
            recv_sem=arrive.at[n, r], device_id=neighbours[way], device_id_type=MESH,
        )

    def key_hop(n):
        way = TREE[n][2] ^ 1
        return pltpu.make_async_remote_copy(
            src_ref=keys.at[TREE[n][1], core], dst_ref=keys.at[n, core], send_sem=key_send.at[n],
            recv_sem=key_arrive.at[n], device_id=neighbours[way], device_id_type=MESH,
        )

    def across(n, r):
        return pltpu.make_async_remote_copy(
            src_ref=part(n, r, core), dst_ref=part(n, r, core), send_sem=send_sib.at[n, r],
            recv_sem=arrive_sib.at[n, r], device_id=sibling, device_id_type=MESH,
        )

    def key_across(n):
        return pltpu.make_async_remote_copy(
            src_ref=keys.at[n, core], dst_ref=keys.at[n, core], send_sem=key_send_sib.at[n],
            recv_sem=key_arrive_sib.at[n], device_id=sibling, device_id_type=MESH,
        )

    barrier = pltpu.get_barrier_semaphore()
    for device_id in neighbours + [sibling]:
        pl.semaphore_signal(barrier, inc=1, device_id=device_id, device_id_type=MESH)

    keys[0, core, 0:1, :] = cluster_ref[...].astype(jnp.float32)
    keys[0, core, 1:2, :] = rank_ref[...].astype(jnp.float32)

    def unit(r):
        wide = x_ref[pl.ds(r * PART, PART), :].astype(jnp.float32)
        scale = 1.0 / jnp.sqrt(jnp.sum(wide * wide, axis=1, keepdims=True) + 1e-06)
        rows[0, pl.ds(pl.multiple_of(r * 2 * PART + core * PART, PART), PART), :] = (wide * scale).astype(jnp.bfloat16)

    unit(0)
    pl.semaphore_wait(barrier, len(neighbours) + 1)
    for m in children[0]:
        key_hop(m).start()
    key_across(0).start()
    for r in range(CHUNKS):
        if r:
            unit(r)
        for m in children[0]:
            if TREE[m][3] == 1:
                hop(m, r).start()
        across(0, r).start()
    for m in children[0]:
        if TREE[m][3] == 2:
            for r in range(CHUNKS):
                hop(m, r).start()

    row_best[...] = jnp.full_like(row_best, -1.0)
    col_best[...] = jnp.full_like(col_best, -1.0)

    def columns_of(n):
        for g in range(CHIP // 128):
            r, which = g // 2, g % 2
            for k in range(2):
                line = keys[n, which, k : k + 1, r * PART : (r + 1) * PART]
                columns[left[n], k, g * 128 : (g + 1) * 128, :] = jnp.broadcast_to(line, (128, 128)).T

    def take(n, r):
        if n:
            hop(n, r).wait_recv()
            if r == 0:
                key_hop(n).wait_recv()
                for m in children[n]:
                    key_hop(m).start()
                key_across(n).start()
            for m in children[n]:
                hop(m, r).start()
            across(n, r).start()

    def take_across(n, r):
        across(n, r).wait_recv()
        if r == 0:
            key_across(n).wait_recv()

    bits = [jnp.int32(0), x // 2, y // 2, z // 2]

    def job(code):
        s, t, h, axis = code % 16, code // 16 % 16, code // 256 % 2, code // 512 % 4
        turn = sum((axis == k).astype(jnp.int32) * bits[k] for k in range(1, 4))
        lhs, rhs = s + turn * (t - s), t + turn * (s - t)
        half = h + turn
        own = (s == t).astype(jnp.int32)
        col = rhs + own * (SLOTS - rhs)
        base = pl.multiple_of(half * ROWS, ROWS)
        score = lax.dot_general(
            rows[lhs], rows[rhs, pl.ds(base, ROWS), :], (((1,), (1,)), ((), ())),
            preferred_element_type=jnp.float32,
        )
        return lhs, rhs, half, col, score

    def keep(lhs, rhs, half, col, score):
        cluster, rank = columns[lhs, 0], columns[lhs, 1]
        best = row_best[lhs]
        for q in range(ROWS // 128):
            line = pl.ds(pl.multiple_of((half * 2 + q // 2) * PART, PART), PART)
            cluster_j = keys[rhs, q % 2, 0:1, line]
            rank_j = keys[rhs, q % 2, 1:2, line]
            same = jnp.where(cluster == cluster_j, score[:, q * 128 : (q + 1) * 128], -1.0)
            later = rank > rank_j
            best = jnp.maximum(best, jnp.where(later, same, -1.0))
            back = jnp.max(jnp.where(later, -1.0, same).reshape(CHIP // 8, 8, 128), axis=0)
            lanes = pl.ds(pl.multiple_of(half * ROWS + q * 128, 128), 128)
            col_best[col, :, lanes] = jnp.maximum(col_best[col, :, lanes], back)
        row_best[lhs] = best

    def encode(entry):
        _, s, t, h, axis = entry
        return s + 16 * t + 256 * h + 512 * axis

    firsts = [[encode(jobs[c][0]) for _, jobs in steps] for c in range(2)]
    seconds = [[encode(jobs[c][1]) for _, jobs in steps] for c in range(2)]

    def pick(i, table):
        code = jnp.int32(0)
        for k in range(len(steps)):
            hit = (i == k).astype(jnp.int32)
            code = code + hit * (table[0][k] + core * (table[1][k] - table[0][k]))
        return code

    def body(i, carry):
        done = {0}
        for k, (arrived, jobs) in enumerate(steps):
            new = [s for pair in jobs for _, s, t, _, axis in pair for s in ((s, t) if axis else (s,)) if s not in done]
            new = sorted(set(new))
            done.update(new)
            if arrived or new or k == 0:

                @pl.when(i == k)
                def _(arrived=arrived, new=new, k=k):
                    for n, r in arrived:
                        take(n, r)
                    if k == 0:
                        for r in range(CHUNKS):
                            take_across(0, r)
                        columns_of(0)
                    for n, r in arrived:
                        take_across(n, r)
                    for n in new:
                        columns_of(n)

        one, two = job(pick(i, firsts)), job(pick(i, seconds))
        keep(*one)
        keep(*two)
        return carry

    lax.fori_loop(0, len(steps), body, 0)

    def back(n, which, target):
        return pltpu.make_async_remote_copy(
            src_ref=outbox.at[n, which], dst_ref=inbox.at[n, core], send_sem=back_send.at[n, which],
            recv_sem=back_arrive.at[n, core], device_id=target, device_id_type=MESH,
        )

    def back_wait(n, which):
        pltpu.make_async_remote_copy(
            src_ref=outbox.at[n, which], dst_ref=inbox.at[n, which], send_sem=back_send.at[n, which],
            recv_sem=back_arrive.at[n, which], device_id=sibling, device_id_type=MESH,
        ).wait_recv()

    for n in list(range(1, SLOTS)) + [0]:
        for g in range(CHIP // 128):
            r, which = g // 2, g % 2
            best = jnp.max(col_best[n, :, g * 128 : (g + 1) * 128], axis=0, keepdims=True)
            if n in left:
                mine = row_best[left[n], g * 128 : (g + 1) * 128, :].T
                best = jnp.maximum(best, jnp.max(mine, axis=0, keepdims=True))
            outbox[n, which, r : r + 1, :] = best
        if n:
            for which in range(2):
                back(n, which, device(OFFSET[n], which)).start()
        else:
            back(0, other, sibling).start()

    total = outbox[0, core]
    for n in range(1, SLOTS):
        for which in range(2):
            back_wait(n, which)
            total = jnp.maximum(total, inbox[n, which])
    back_wait(0, other)
    out_ref[...] = jnp.maximum(total, inbox[0, other])

    for n in range(SLOTS):
        for r in range(CHUNKS):
            across(n, r).wait_send()
            if n:
                hop(n, r).wait_send()
        key_across(n).wait_send()
        if n:
            key_hop(n).wait_send()
            for which in range(2):
                back(n, which, sibling).wait_send()
        else:
            back(0, other, sibling).wait_send()


def local(embeddings, cluster_ids, priority):
    steps, late = plan()
    assert not late
    left = sorted({s for _, jobs in steps for pair in jobs for _, s, t, _, axis in pair for s in ((s, t) if axis else (s,))})
    assert left == list(range(len(left)))
    left = {n: n for n in left}
    dma = pltpu.SemaphoreType.DMA
    best = pl.pallas_call(
        functools.partial(kernel, steps, left),
        out_shape=jax.ShapeDtypeStruct((CHUNKS, PART), jnp.float32),
        in_specs=[pl.BlockSpec(memory_space=pltpu.VMEM)] * 3,
        out_specs=pl.BlockSpec(memory_space=pltpu.VMEM),
        scratch_shapes=[
            pltpu.VMEM((SLOTS, CHIP, WIDTH), jnp.bfloat16),
            pltpu.VMEM((SLOTS, 2, 2, ROWS), jnp.float32),
            pltpu.VMEM((len(left), 2, CHIP, 128), jnp.float32),
            pltpu.VMEM((len(left), CHIP, 128), jnp.float32),
            pltpu.VMEM((SLOTS + 1, 8, CHIP), jnp.float32),
            pltpu.VMEM((SLOTS, 2, CHUNKS, PART), jnp.float32),
            pltpu.VMEM((SLOTS, 2, CHUNKS, PART), jnp.float32),
            dma((SLOTS, CHUNKS)),
            dma((SLOTS, CHUNKS)),
            dma((SLOTS, CHUNKS)),
            dma((SLOTS, CHUNKS)),
            dma((SLOTS,)),
            dma((SLOTS,)),
            dma((SLOTS,)),
            dma((SLOTS,)),
            dma((SLOTS, 2)),
            dma((SLOTS, 2)),
        ],
        compiler_params=pltpu.CompilerParams(
            collective_id=0, has_side_effects=True, vmem_limit_bytes=60 * 2**20
        ),
    )(embeddings, cluster_ids.reshape(1, ROWS), priority.reshape(1, ROWS))
    return best.reshape(ROWS)


def solution(mesh):
    placed = (P(("grp", "blk"), None), P(("grp", "blk"), None), P(("grp", "blk")))
    return jax.shard_map(
        local, mesh=mesh, in_specs=placed, out_specs=P(("grp", "blk")), check_vma=False
    )
```

time: 298 us -> 126 us (0.42)
  waiting for transfers between devices: 134 us -> 0 us
  Pallas kernels: 0 us -> 125 us
  blocking collectives: 81.5 us -> 0 us
  matrix products: 40.3 us -> 0 us
  between operations: 13.5 us -> 0.01 us
  other arithmetic: 12.2 us -> 0 us
  local copies, waits for them, and re-layouts: 9.02 us -> 1.26 us
  starting transfers between devices: 7.45 us -> 0 us
    all_gather x1 -> x0, waiting for transfers between devices: 127 us -> none  [local(): lax.all_gather(query, 'blk', axis=0, tiled=True)]
    pallas_call x0 -> x1, Pallas kernels: none -> 125 us  [local(): pl.pallas_call(functools.partial(kernel, steps, left), out_shape=jax.Shap...]
    all_to_all x2 -> x0, blocking collectives: 70 us -> none  [the longest x1 59.3 us: local(): lax.all_to_all(outbox.reshape(groups, slots, width), 'grp', split_axis=0,...]
    dot_general x1 -> x0, matrix products: 40.3 us -> none  [local(): lax.dot_general(query, lax.all_gather(query, 'blk', axis=0, tiled=True),...]
    all_gather x1 -> x0, blocking collectives: 11.5 us -> none  [local(): lax.all_gather(q_rank, 'blk', axis=0, tiled=True)[None, :] < q_rank[:, None]]
    all_to_all x1 -> x0, starting transfers between devices: 7.45 us -> none  [local(): lax.all_to_all(best_local.reshape(groups, slots), 'grp', split_axis=0, co...]
    all_to_all x1 -> x0, waiting for transfers between devices: 6.93 us -> none  [local(): lax.all_to_all(best_local.reshape(groups, slots), 'grp', split_axis=0, co...]
    scatter x1 -> x0, other arithmetic: 5.95 us -> none  [local(): jnp.zeros((groups * slots, width), jnp.bfloat16).at[target].set(unit)]
  transfers between devices with their start and end apart: 2 -> 0, of which waited for: 2 -> 0; matrix products, arithmetic and copies ran while one was open for 1% -> 0% of each run, Pallas kernels for 0% -> 0%
where the time goes in v1:
time: 126 us
  Pallas kernels  125 us (99%)
  local copies, waits for them, and re-layouts  1.26 us (1%)
    pallas_call x1, Pallas kernels, local(): pl.pallas_call(functools.partial(kernel, steps, left), out_shape=jax.Shap...  125 us

profile of v1, /device:TPU:1, one launch (start us, length us, event | category | flops | bytes accessed | tf_op | source)
XLA Modules:
  0.0 126.2 jit_solution(12862310234317241046)
XLA Ops:
  0.0 124.9 %shard_map.37 = f32[4,128]{1,0:T(4,128)} custom-call(bf16[512,1024]{1,0:T(8,128)(2,1)} %x_ref.1, s32[1,512]{1,0:T(1,128)} %bitcast.4, s32[1,512]{1,0:T(1,128)} %bitcast.5), custom_call_target="tpu_custom_call" | custom-call | tf_op jit(solution)/shard_map/pallas_call | solution.py:346
  124.9 1.3 copy.5

commit v2 on v1

v2 whole, which is shorter than its diff:
```python
import functools

import jax
import jax.numpy as jnp
from jax import lax
from jax.experimental import pallas as pl
from jax.experimental.pallas import tpu as pltpu
from jax.sharding import PartitionSpec as P

MESH = pl.DeviceIdType.MESH
SIDE = 4
CHUNKS = 4
WIDTH = 1024
ROWS = 512
PART = ROWS // CHUNKS
CHIP = 2 * ROWS
STEP = ((1, 0, 0), (-1, 0, 0), (0, 1, 0), (0, -1, 0), (0, 0, 1), (0, 0, -1))

TREE = (
    (0, -1, -1, 0),
    (3, 0, 5, 1),
    (51, 1, 1, 1),
    (4, 0, 2, 1),
    (5, 3, 4, 1),
    (20, 3, 0, 1),
    (12, 0, 3, 1),
    (1, 0, 4, 2),
    (35, 2, 1, 2),
    (23, 5, 5, 2),
    (63, 2, 3, 2),
    (9, 4, 2, 2),
)
SLOTS = len(TREE)
OFFSET = [(v // 16, v // 4 % 4, v % 4) for v, _, _, _ in TREE]

BLOCK_US = 23.0
HOP_US = 0.7
SIBLING_US = 1.5
LOOP_US = 2.5
EAGER_US = 0.8
SHORT_US = 1.55
LONG_US = 2.65


def arrivals():
    start = [0.0] * SLOTS
    for _ in range(SLOTS):
        for n in range(1, SLOTS):
            _, parent, way, wave = TREE[n]
            begin = 0.0 if parent == 0 else start[parent] + BLOCK_US / CHUNKS + HOP_US
            if wave == 2:
                for m in range(1, SLOTS):
                    if TREE[m][2] == way and TREE[m][3] == 1:
                        begin = max(begin, start[m] + BLOCK_US)
            start[n] = begin
    return [
        [0.0 if n == 0 else start[n] + HOP_US + BLOCK_US * (r + 1) / CHUNKS for r in range(CHUNKS)]
        for n in range(SLOTS)
    ]


def choose(ready):
    best = {}
    for s in range(SLOTS):
        for t in range(SLOTS):
            if s == t:
                continue
            d = tuple((a - b) % SIDE for a, b in zip(OFFSET[s], OFFSET[t]))
            e = tuple(-a % SIDE for a in d)
            axis = [k for k in range(3) if d[k] == 2][0] + 1 if d == e else 0
            if axis:
                times = [max(ready[s][-1], ready[t][-1])] * 2
            else:
                times = [max(ready[s][-1], ready[t][r]) for r in range(CHUNKS)]
            cost = sum(a**3 for a in times) / len(times) + (s > 6) * 1e3
            if min(d, e) not in best or cost < best[min(d, e)][0]:
                best[min(d, e)] = (cost, s, t, axis)
    assert len(best) == SIDE**3 // 2 + 3
    return sorted(best.values())


def plan():
    ready = arrivals()
    events = sorted((ready[n][r], n, r) for n in range(1, SLOTS) for r in range(CHUNKS))
    here = {(0, r): 0.0 for r in range(CHUNKS)}
    crossing = []
    pieces = []
    for _, s, t, axis in choose(ready):
        pieces.append((s, t, axis, set(range(2 if axis else CHUNKS))))
    steps = []
    now = LOOP_US
    ops = []

    def advance(until):
        while True:
            a = events[0][0] if events else 1e9
            b = crossing[0][0] if crossing else 1e9
            if min(a - EAGER_US, b) > until:
                return
            if a - EAGER_US <= b:
                when, n, r = events.pop(0)
                ops.append(("take", n, r))
                crossing.append((max(when, now) + SIBLING_US, n, r))
            else:
                when, n, r = crossing.pop(0)
                ops.append(("cross", n, r))
                here[n, r] = when

    def full(n):
        return all((n, r) in here for r in range(CHUNKS))

    steps.append(([], "short", [(0, 0, 0, 0, 1, 0), (0, 0, 2, 0, 3, 0)]))
    now += SHORT_US
    while pieces:
        advance(now)
        whole = [p for p in pieces if not p[2] and len(p[3]) == CHUNKS and full(p[0]) and full(p[1])]
        ready_pieces = []
        for p in pieces:
            s, t, axis, left = p
            if not full(s):
                continue
            if axis:
                if full(t):
                    ready_pieces.append((p, (0, 1)))
                continue
            if p in whole:
                continue
            ready_pieces += [(p, (r,)) for r in sorted(left) if (t, r) in here]
        shorts = []
        by = {}
        for p, rs in ready_pieces:
            if len(rs) == 2:
                shorts.append([(p, 0), (p, 1)])
            else:
                by.setdefault(p[0], []).append((p, rs[0]))
        single = []
        for s, lst in by.items():
            while len(lst) >= 2:
                shorts.append([lst.pop(0), lst.pop(0)])
            if lst:
                single.append([lst[0], lst[0]])
        last = not events and not crossing
        if len(shorts) < 2 and len(whole) < 2 and last:
            shorts += single
            if len(shorts) < 2 and whole:
                p = whole.pop(0)
                shorts += [[(p, 0), (p, 1)], [(p, 2), (p, 3)]]
            if len(shorts) == 1:
                shorts.append(shorts[0])
        if len(whole) >= 2 and (len(shorts) < 2):
            pair = whole[:2]
            steps.append((ops, "long", [(p[0], p[1]) for p in pair]))
            for p in pair:
                pieces.remove(p)
            ops = []
            now += LONG_US
        elif len(shorts) >= 2:
            entry = []
            for body in shorts[:2]:
                (p, r1), (q, r2) = body
                entry.append((p[0], p[1], r1, q[1], r2, p[2]))
                for a, r in body:
                    a[3].discard(r)
            pieces = [p for p in pieces if p[3]]
            steps.append((ops, "short", entry))
            ops = []
            now += SHORT_US
        else:
            nxt = min([e[0] for e in events[:1]] + [c[0] for c in crossing[:1]])
            now = max(now, nxt)
    assert not events
    while crossing:
        when, n, r = crossing.pop(0)
        ops.append(("cross", n, r))
    return steps, ops, now, ready


def sends(steps):
    waiting, sent = [], set()

    def follow(n, r):
        waiting.extend((m, r) for m in range(1, SLOTS) if TREE[m][1] == n)
        out = []
        for m, q in sorted(waiting, key=lambda a: TREE[a[0]][3]):
            ahead = [w for w in range(1, SLOTS) if TREE[w][2] == TREE[m][2] and TREE[w][3] == 1 and TREE[m][3] == 2]
            if all((w, c) in sent for w in ahead for c in range(CHUNKS)):
                sent.add((m, q))
                waiting.remove((m, q))
                out.append((m, q))
        return out

    first = [follow(0, r) for r in range(CHUNKS)]
    for ops, _, _ in steps:
        for k, op in enumerate(ops):
            if op[0] == "take":
                ops[k] = (*op, follow(op[1], op[2]))
    assert not waiting
    return first


def schedule():
    steps, rest, _, _ = plan()
    last, made = {}, set()
    for k, (_, _, jobs) in enumerate(steps):
        for job in jobs:
            s, others = job[0], (job[1::2] if len(job) == 2 else (job[1], job[3]))
            for n in (s, *others):
                last[n] = k
    out = []
    for k, (ops, kind, jobs) in enumerate(steps):
        ops = list(ops)
        for job in jobs:
            swap = (job[1], job[3]) if len(job) > 2 and job[5] else ()
            for n in (job[0], *swap):
                if n not in made:
                    made.add(n)
                    ops.append(("columns", n))
        ops += [("flush", n) for n in range(SLOTS) if last[n] == k - 1]
        out.append((ops, kind, jobs))
    first = sends(out + [(rest, "", ())])
    return first, out, list(rest) + [("flush", n) for n in range(SLOTS) if last[n] == len(steps) - 1], made


def kernel(first, steps, rest, made, x_ref, cluster_ref, rank_ref, out_ref, rows, keys, columns, row_best, col_best, outbox,
           inbox, send, arrive, send_sib, arrive_sib, key_send, key_arrive, key_send_sib, key_arrive_sib,
           back_send, back_arrive):
    grp, z = lax.axis_index("grp"), lax.axis_index("blk")
    x, y, core = grp // (2 * SIDE), grp // 2 % SIDE, grp % 2
    other = 1 - core

    def device(offset, which):
        dx, dy, dz = offset
        return (
            (x + dx + SIDE) % SIDE * (2 * SIDE) + (y + dy + SIDE) % SIDE * 2 + which,
            (z + dz + SIDE) % SIDE,
        )

    neighbours = [device(step, core) for step in STEP]
    sibling = device((0, 0, 0), other)

    def part(n, r, which):
        return rows.at[n, pl.ds(pl.multiple_of(r * 2 * PART + which * PART, PART), PART)]

    def hop(n, r):
        way = TREE[n][2] ^ 1
        return pltpu.make_async_remote_copy(
            src_ref=part(TREE[n][1], r, core), dst_ref=part(n, r, core), send_sem=send.at[n, r],
            recv_sem=arrive.at[n, r], device_id=neighbours[way], device_id_type=MESH,
        )

    def key_hop(n):
        way = TREE[n][2] ^ 1
        return pltpu.make_async_remote_copy(
            src_ref=keys.at[TREE[n][1], core], dst_ref=keys.at[n, core], send_sem=key_send.at[n],
            recv_sem=key_arrive.at[n], device_id=neighbours[way], device_id_type=MESH,
        )

    def across(n, r):
        return pltpu.make_async_remote_copy(
            src_ref=part(n, r, core), dst_ref=part(n, r, core), send_sem=send_sib.at[n, r],
            recv_sem=arrive_sib.at[n, r], device_id=sibling, device_id_type=MESH,
        )

    def key_across(n):
        return pltpu.make_async_remote_copy(
            src_ref=keys.at[n, core], dst_ref=keys.at[n, core], send_sem=key_send_sib.at[n],
            recv_sem=key_arrive_sib.at[n], device_id=sibling, device_id_type=MESH,
        )

    def forward(pairs):
        for n, r in pairs:
            hop(n, r).start()
            if r == 0:
                key_hop(n).start()

    barrier = pltpu.get_barrier_semaphore()
    for device_id in neighbours + [sibling]:
        pl.semaphore_signal(barrier, inc=1, device_id=device_id, device_id_type=MESH)

    keys[0, core, 0:1, :] = cluster_ref[...].astype(jnp.float32)
    keys[0, core, 1:2, :] = rank_ref[...].astype(jnp.float32)

    def unit(r):
        wide = x_ref[pl.ds(r * PART, PART), :].astype(jnp.float32)
        scale = 1.0 / jnp.sqrt(jnp.sum(wide * wide, axis=1, keepdims=True) + 1e-06)
        rows[0, pl.ds(pl.multiple_of(r * 2 * PART + core * PART, PART), PART), :] = (wide * scale).astype(jnp.bfloat16)

    unit(0)
    pl.semaphore_wait(barrier, len(neighbours) + 1)
    key_across(0).start()
    for r in range(CHUNKS):
        if r:
            unit(r)
        forward(first[r])
        across(0, r).start()

    row_best[...] = jnp.full_like(row_best, -1.0)
    col_best[...] = jnp.full_like(col_best, -1.0)

    def columns_of(n):
        for g in range(CHIP // 128):
            r, which = g // 2, g % 2
            for k in range(2):
                line = keys[n, which, k : k + 1, r * PART : (r + 1) * PART]
                columns[n, k, g * 128 : (g + 1) * 128, :] = jnp.broadcast_to(line, (128, 128)).T

    def take(n, r, follow):
        if r == 0:
            key_hop(n).wait_recv()
        hop(n, r).wait_recv()
        forward(follow)
        if r == 0:
            key_across(n).start()
        across(n, r).start()

    def cross(n, r):
        across(n, r).wait_recv()
        if r == 0:
            key_across(n).wait_recv()

    def back(n, which, target):
        return pltpu.make_async_remote_copy(
            src_ref=outbox.at[n, which], dst_ref=inbox.at[n, core], send_sem=back_send.at[n, which],
            recv_sem=back_arrive.at[n, core], device_id=target, device_id_type=MESH,
        )

    def back_wait(n, which):
        pltpu.make_async_remote_copy(
            src_ref=outbox.at[n, which], dst_ref=inbox.at[n, which], send_sem=back_send.at[n, which],
            recv_sem=back_arrive.at[n, which], device_id=sibling, device_id_type=MESH,
        ).wait_recv()

    def flush(n):
        for g in range(CHIP // 128):
            r, which = g // 2, g % 2
            best = jnp.max(col_best[n, :, g * 128 : (g + 1) * 128], axis=0, keepdims=True)
            if n in made:
                mine = row_best[n, g * 128 : (g + 1) * 128, :].T
                best = jnp.maximum(best, jnp.max(mine, axis=0, keepdims=True))
            outbox[n, which, r : r + 1, :] = best
        if n:
            for which in range(2):
                back(n, which, device(OFFSET[n], which)).start()
        else:
            back(0, other, sibling).start()

    def run(op):
        {"take": take, "cross": cross, "columns": columns_of, "flush": flush}[op[0]](*op[1:])

    bits = [jnp.int32(0), x // 2, y // 2, z // 2]

    def keep(lhs, rhs, col, base, score):
        cluster, rank = columns[lhs, 0], columns[lhs, 1]
        best = row_best[lhs]
        for q in range(score.shape[1] // 128):
            line = pl.ds(pl.multiple_of(base // 2 + q // 2 * PART, PART), PART)
            cluster_j = keys[rhs, q % 2, 0:1, line]
            rank_j = keys[rhs, q % 2, 1:2, line]
            same = jnp.where(cluster == cluster_j, score[:, q * 128 : (q + 1) * 128], -1.0)
            later = rank > rank_j
            best = jnp.maximum(best, jnp.where(later, same, -1.0))
            back = jnp.max(jnp.where(later, -1.0, same).reshape(CHIP // 8, 8, 128), axis=0)
            lanes = pl.ds(pl.multiple_of(base + q * 128, 128), 128)
            col_best[col, :, lanes] = jnp.maximum(col_best[col, :, lanes], back)
        row_best[lhs] = best

    def product(lhs, rhs, base, width):
        return lax.dot_general(
            rows[lhs], rows[rhs, pl.ds(base, width), :], (((1,), (1,)), ((), ())),
            preferred_element_type=jnp.float32,
        )

    def short(code):
        s, t1, r1, t2, r2, axis = (code // d % m for d, m in ((1, 16), (16, 16), (256, 4), (1024, 16), (16384, 4), (65536, 4)))
        turn = sum((axis == k).astype(jnp.int32) * bits[k] for k in range(1, 4))
        lhs = s + turn * (t1 - s)
        todo = []
        for t, r in ((t1, r1), (t2, r2)):
            rhs = t + turn * (s - t)
            base = pl.multiple_of((r + 2 * turn) * 2 * PART, 2 * PART)
            col = rhs + (s == t).astype(jnp.int32) * (SLOTS - rhs)
            todo.append((rhs, col, base, product(lhs, rhs, base, 2 * PART)))
        for rhs, col, base, score in todo:
            keep(lhs, rhs, col, base, score)

    def long(code):
        s, t = code % 16, code // 16 % 16
        keep(s, t, t, 0, product(s, t, 0, CHIP))

    def encode(job):
        scale = (1, 16, 256, 1024, 16384, 65536)
        return sum(a * b for a, b in zip(job, scale))

    def body(i, carry):
        code, wide = jnp.int32(0), jnp.int32(0)
        for k, (ops, kind, jobs) in enumerate(steps):
            one, two = encode(jobs[0]), encode(jobs[1])
            hit = (i == k).astype(jnp.int32)
            code = code + hit * (one + core * (two - one))
            if kind == "long":
                wide = wide + hit
            if ops:

                @pl.when(i == k)
                def _(ops=ops):
                    for op in ops:
                        run(op)

        @pl.when(wide == 0)
        def _():
            short(code)

        @pl.when(wide == 1)
        def _():
            long(code)

        return carry

    for r in range(CHUNKS):
        cross(0, r)
    lax.fori_loop(0, len(steps), body, 0)
    for op in rest:
        run(op)
    for n in range(SLOTS):
        for r in range(CHUNKS):
            across(n, r).wait_send()
            if n:
                hop(n, r).wait_send()
        key_across(n).wait_send()
        if n:
            key_hop(n).wait_send()

    total = outbox[0, core]
    for n in range(1, SLOTS):
        for which in range(2):
            back_wait(n, which)
            total = jnp.maximum(total, inbox[n, which])
    back_wait(0, other)
    out_ref[...] = jnp.maximum(total, inbox[0, other])
    for n in range(1, SLOTS):
        for which in range(2):
            back(n, which, sibling).wait_send()
    back(0, other, sibling).wait_send()


def local(embeddings, cluster_ids, priority):
    first, steps, rest, made = schedule()
    dma = pltpu.SemaphoreType.DMA
    best = pl.pallas_call(
        functools.partial(kernel, first, steps, rest, made),
        out_shape=jax.ShapeDtypeStruct((CHUNKS, PART), jnp.float32),
        in_specs=[pl.BlockSpec(memory_space=pltpu.VMEM)] * 3,
        out_specs=pl.BlockSpec(memory_space=pltpu.VMEM),
        scratch_shapes=[
            pltpu.VMEM((SLOTS, CHIP, WIDTH), jnp.bfloat16),
            pltpu.VMEM((SLOTS, 2, 2, ROWS), jnp.float32),
            pltpu.VMEM((SLOTS, 2, CHIP, 128), jnp.float32),
            pltpu.VMEM((SLOTS, CHIP, 128), jnp.float32),
            pltpu.VMEM((SLOTS + 1, 8, CHIP), jnp.float32),
            pltpu.VMEM((SLOTS, 2, CHUNKS, PART), jnp.float32),
            pltpu.VMEM((SLOTS, 2, CHUNKS, PART), jnp.float32),
            dma((SLOTS, CHUNKS)),
            dma((SLOTS, CHUNKS)),
            dma((SLOTS, CHUNKS)),
            dma((SLOTS, CHUNKS)),
            dma((SLOTS,)),
            dma((SLOTS,)),
            dma((SLOTS,)),
            dma((SLOTS,)),
            dma((SLOTS, 2)),
            dma((SLOTS, 2)),
        ],
        compiler_params=pltpu.CompilerParams(
            collective_id=0, has_side_effects=True, vmem_limit_bytes=60 * 2**20
        ),
    )(embeddings, cluster_ids.reshape(1, ROWS), priority.reshape(1, ROWS))
    return best.reshape(ROWS)


def solution(mesh):
    placed = (P(("grp", "blk"), None), P(("grp", "blk"), None), P(("grp", "blk")))
    return jax.shard_map(
        local, mesh=mesh, in_specs=placed, out_specs=P(("grp", "blk")), check_vma=False
    )
```

time: 126 us -> 102 us (0.81)
  Pallas kernels: 125 us -> 101 us
    pallas_call x1, Pallas kernels: 125 us -> 101 us  [local(): pl.pallas_call(functools.partial(kernel, first, steps, rest, made), out_s...]
where the time goes in v2:
time: 102 us
  Pallas kernels  101 us (99%)
  local copies, waits for them, and re-layouts  1.26 us (1%)
    pallas_call x1, Pallas kernels, local(): pl.pallas_call(functools.partial(kernel, first, steps, rest, made), out_s...  101 us

profile of v2, /device:TPU:1, one launch (start us, length us, event | category | flops | bytes accessed | tf_op | source)
XLA Modules:
  0.0 102.1 jit_solution(15595627228890310946)
XLA Ops:
  0.0 100.8 %shard_map.37 = f32[4,128]{1,0:T(4,128)} custom-call(bf16[512,1024]{1,0:T(8,128)(2,1)} %x_ref.1, s32[1,512]{1,0:T(1,128)} %bitcast.4, s32[1,512]{1,0:T(1,128)} %bitcast.5), custom_call_target="tpu_custom_call" | custom-call | tf_op jit(solution)/shard_map/pallas_call | solution.py:449
  100.8 1.3 %copy.5 = f32[512]{0:T(512)} copy(f32[512]{0:T(512)} %bitcast.3) | data formatting | bytes 4096

commit v3 on v2

v3 whole, which is shorter than its diff:
```python
import functools

import jax
import jax.numpy as jnp
from jax import lax
from jax.experimental import pallas as pl
from jax.experimental.pallas import tpu as pltpu
from jax.sharding import PartitionSpec as P

MESH = pl.DeviceIdType.MESH
SIDE = 4
CHUNKS = 4
WIDTH = 1024
ROWS = 512
PART = ROWS // CHUNKS
CHIP = 2 * ROWS
STEP = ((1, 0, 0), (-1, 0, 0), (0, 1, 0), (0, -1, 0), (0, 0, 1), (0, 0, -1))

TREE = (
    (0, -1, -1, 0),
    (3, 0, 5, 1),
    (12, 0, 3, 1),
    (16, 0, 0, 1),
    (20, 3, 2, 1),
    (13, 2, 4, 1),
    (48, 0, 1, 1),
    (51, 1, 1, 2),
    (9, 5, 3, 2),
    (50, 7, 5, 2),
    (21, 4, 4, 2),
    (24, 4, 2, 2),
)
SLOTS = len(TREE)
OFFSET = [(v // 16, v // 4 % 4, v % 4) for v, _, _, _ in TREE]

QUARTERS = 4
GROUP = 6
BLOCK_US = 23.0
HOP_US = 0.8
CROSS_US = 1.5
LOOP_US = 2.5
EAGER_US = 0.8
EARLY_US = 12.0
BODY_US = {"short": 1.55, "half": 1.55, "long": 2.65}
OP_US = {"take": 0.15, "cross": 0.06, "columns": 0.35, "flush": 0.3}


def covers(n, r):
    return (2 * r, 2 * r + 1) if TREE[n][3] == 2 else (r,)


def copies(n):
    return 2 if TREE[n][3] == 2 else QUARTERS


def first_on_link(m):
    return [w for w in range(1, SLOTS) if TREE[m][3] == 2 and TREE[w][2] == TREE[m][2] and TREE[w][3] == 1]


def arrivals():
    at = {(0, r): 0.0 for r in range(QUARTERS)}
    free = {}
    for wave in (1, 2):
        todo = [n for n in range(1, SLOTS) if TREE[n][3] == wave]
        for _ in range(SLOTS):
            for n in list(todo):
                parent, way = TREE[n][1], TREE[n][2]
                if parent and (parent, 0) not in at:
                    continue
                clock = max([free.get(way, 0.0)])
                for r in range(copies(n)):
                    need = [c for c in range(copies(parent)) if set(covers(parent, c)) & set(covers(n, r))] if parent else []
                    clock = max([clock] + [at[parent, c] for c in need]) + BLOCK_US / copies(n)
                    at[n, r] = clock + HOP_US
                free[way] = clock
                todo.remove(n)
    return at


def choose(at):
    full = [max(at[n, r] for r in range(copies(n))) for n in range(SLOTS)]
    best = {}
    for s in range(SLOTS):
        for t in range(SLOTS):
            if s == t:
                continue
            d = tuple((a - b) % SIDE for a, b in zip(OFFSET[s], OFFSET[t]))
            e = tuple(-a % SIDE for a in d)
            axis = [k for k in range(3) if d[k] == 2][0] + 1 if d == e else 0
            cost = max(full[s], full[t]), full[s], s
            if min(d, e) not in best or cost < best[min(d, e)][0]:
                best[min(d, e)] = (cost, s, t, axis)
    assert len(best) == SIDE**3 // 2 + 3
    return [b[1:] for b in sorted(best.values())]


def plan():
    at = arrivals()
    events = sorted((when, n, r) for (n, r), when in at.items() if n)
    assert len(at) == QUARTERS + sum(copies(n) for n in range(1, SLOTS))
    crossing = []
    here = {(0, q) for q in range(QUARTERS)}
    todo = [[s, t, axis, None] for s, t, axis in choose(at)]
    steps = [[[], "short", [(0, 0, 0, 0, 1, 0), (0, 0, 2, 0, 3, 0)]]]
    made = {0}
    now = LOOP_US + BODY_US["short"]
    ops = []

    def advance():
        nonlocal now
        while True:
            a = events[0][0] if events else 1e9
            b = crossing[0][0] if crossing else 1e9
            if min(a - EAGER_US, b) > now:
                return
            if a - EAGER_US <= b:
                _, n, r = events.pop(0)
                ops.append(("take", n, r))
                now += OP_US["take"]
                crossing.append((now + CROSS_US, n, r))
            else:
                _, n, r = crossing.pop(0)
                ops.append(("cross", n, r))
                now += OP_US["cross"]
                here.update((n, q) for q in covers(n, r))

    def full(n):
        return all((n, q) in here for q in range(QUARTERS))

    def drained():
        return not events and not crossing

    def half(n, h):
        return (n, 2 * h) in here and (n, 2 * h + 1) in here

    for _ in range(400):
        if not todo:
            break
        advance()
        longs, lone, columns, cells = [], [], {}, {}
        for c in todo:
            s, t, axis, left = c
            if axis:
                if full(s) and full(t):
                    lone.append((c, None, (s, t, 0, t, 1, axis)))
            elif left is None and full(s) and full(t):
                longs.append(c)
            else:
                if full(s) and (left is None and (s == 0 and now < EARLY_US or drained()) or left is not None and left[0] == "short"):
                    for q in range(QUARTERS):
                        if (t, q) in here and (left is None or q in left[1]):
                            columns.setdefault(s, []).append((c, q))
                if left is None and (now < EARLY_US or drained()) or left is not None and left[0] == "half":
                    for a in range(2):
                        for b in range(2):
                            if half(s, a) and half(t, b) and (left is None or (a, b) in left[1]):
                                cells.setdefault((s, a), []).append((c, (a, b)))
        shorts, halves, odd_shorts, odd_halves = [], [], [], []
        for s, found in columns.items():
            for k in range(0, len(found), 2):
                p = found[k : k + 2]
                (odd_shorts if len(p) == 1 else shorts).append(p)
        shorts += lone
        for key, found in cells.items():
            for k in range(0, len(found), 2):
                p = found[k : k + 2]
                (odd_halves if len(p) == 1 else halves).append(p)
        soon = min([e[0] for e in events[:1]] + [c[0] for c in crossing[:1]] + [1e9]) - now
        kind = None
        if len(longs) >= 2:
            kind, entry = "long", [(c[0], c[1]) for c in longs[:2]]
            for c in longs[:2]:
                todo.remove(c)
        elif len(shorts) >= 2 or (len(halves) < 2 and (len(shorts) + len(longs)) and soon > 0.8):
            bodies = shorts[:2]
            if len(bodies) < 2 and longs:
                c = longs[0]
                bodies = bodies + [[(c, 0), (c, 1)], [(c, 2), (c, 3)]]
                bodies = bodies[:2]
            if len(bodies) < 2 and odd_shorts:
                bodies.append(odd_shorts[0] * 2)
            if len(bodies) < 2:
                bodies = bodies * 2
            kind, entry = "short", []
            for body in bodies:
                if isinstance(body, tuple):
                    entry.append(body[2])
                    if body[0] in todo:
                        todo.remove(body[0])
                    continue
                (c, q), (d, p) = body
                entry.append((c[0], c[1], q, d[1], p, 0))
                for e, r in body:
                    if e[3] is None:
                        e[3] = ("short", set(range(QUARTERS)))
                    e[3][1].discard(r)
        elif len(halves) >= 2 or ((halves or odd_halves or odd_shorts) and (drained() or soon > 0.8)):
            if not halves and not odd_halves:
                kind, bodies = "short", (odd_shorts * 2)[:2]
                bodies = [b * 2 for b in bodies]
            else:
                kind, bodies = "half", (halves + [b * 2 for b in odd_halves])[:2]
                bodies = (bodies * 2)[:2]
            entry = []
            for (c, q), (d, p) in bodies:
                if kind == "half":
                    entry.append((c[0], c[1], q[1], d[1], p[1], q[0]))
                else:
                    entry.append((c[0], c[1], q, d[1], p, 0))
                for e, r in ((c, q), (d, p)):
                    if e[3] is None:
                        e[3] = (kind, {(a, b) for a in range(2) for b in range(2)} if kind == "half" else set(range(QUARTERS)))
                    e[3][1].discard(r)
        if kind is None:
            now += max(soon, 0.01)
            continue
        todo = [c for c in todo if c[3] is None or c[3][1]]
        for job in entry:
            lefts = [job[0]] + ([job[1]] if kind == "short" and job[5] else [])
            for n in lefts:
                if n not in made:
                    made.add(n)
                    ops.append(("columns", n))
                    now += OP_US["columns"]
        steps.append([ops, kind, entry])
        ops = []
        now += BODY_US[kind]
    assert not events and not todo
    rest = ops + [("cross", n, r) for _, n, r in crossing]
    last = {}
    for k, (_, _, entry) in enumerate(steps):
        for job in entry:
            for n in (job[0], job[1], *(job[3:4])):
                last[n] = k
    ends = len(steps) - 1
    for n in range(SLOTS):
        if last[n] == ends:
            rest.append(("flush", n))
        else:
            steps[last[n] + 1][0].append(("flush", n))
    return steps, rest, made, now


def sends(steps):
    have, sent = {n: set() for n in range(SLOTS)}, set()

    def follow(n, r):
        have[n].update(covers(n, r))
        out = []
        for m in sorted(range(1, SLOTS), key=lambda k: TREE[k][3]):
            for q in range(copies(m)):
                ahead = {(w, c) for w in first_on_link(m) for c in range(copies(w))}
                if (m, q) not in sent and set(covers(m, q)) <= have[TREE[m][1]] and ahead <= sent:
                    sent.add((m, q))
                    out.append((m, q))
        return out

    first = [follow(0, r) for r in range(QUARTERS)]
    for ops, _, _ in steps:
        for k, op in enumerate(ops):
            if op[0] == "take":
                ops[k] = (*op, follow(op[1], op[2]))
    assert len(sent) == sum(copies(n) for n in range(1, SLOTS))
    return first


def kernel(first, steps, rest, made, x_ref, cluster_ref, rank_ref, out_ref, rows, keys, columns, row_best, col_best, outbox,
           inbox, send, arrive, send_sib, arrive_sib, key_send, key_arrive, key_send_sib, key_arrive_sib,
           back_send, back_arrive):
    grp, z = lax.axis_index("grp"), lax.axis_index("blk")
    x, y, core = grp // (2 * SIDE), grp // 2 % SIDE, grp % 2
    other = 1 - core
    along_x = [lax.rem(x + d, SIDE) * (2 * SIDE) for d in range(SIDE)]
    along_y = [lax.rem(y + d, SIDE) * 2 for d in range(SIDE)]
    along_z = [lax.rem(z + d, SIDE) for d in range(SIDE)]

    def device(offset, which):
        dx, dy, dz = offset
        return along_x[dx % SIDE] + along_y[dy % SIDE] + which, along_z[dz % SIDE]

    neighbours = [device(step, core) for step in STEP]
    sibling = device((0, 0, 0), other)

    def part(n, r, which, slot=None):
        slot = n if slot is None else slot
        if copies(n) == 2:
            return rows.at[slot, pl.ds(2 * r, 2), which]
        return rows.at[slot, r, which]

    def hop(n, r):
        way = TREE[n][2] ^ 1
        return pltpu.make_async_remote_copy(
            src_ref=part(n, r, core, TREE[n][1]), dst_ref=part(n, r, core), send_sem=send.at[n, r],
            recv_sem=arrive.at[n, r], device_id=neighbours[way], device_id_type=MESH,
        )

    def key_hop(n):
        way = TREE[n][2] ^ 1
        return pltpu.make_async_remote_copy(
            src_ref=keys.at[TREE[n][1], core], dst_ref=keys.at[n, core], send_sem=key_send.at[n],
            recv_sem=key_arrive.at[n], device_id=neighbours[way], device_id_type=MESH,
        )

    def across(n, r):
        return pltpu.make_async_remote_copy(
            src_ref=part(n, r, core), dst_ref=part(n, r, core), send_sem=send_sib.at[n, r],
            recv_sem=arrive_sib.at[n, r], device_id=sibling, device_id_type=MESH,
        )

    def key_across(n):
        return pltpu.make_async_remote_copy(
            src_ref=keys.at[n, core], dst_ref=keys.at[n, core], send_sem=key_send_sib.at[n],
            recv_sem=key_arrive_sib.at[n], device_id=sibling, device_id_type=MESH,
        )

    def forward(pairs):
        for n, r in pairs:
            hop(n, r).start()
            if r == 0:
                key_hop(n).start()

    barrier = pltpu.get_barrier_semaphore()
    for device_id in neighbours + [sibling]:
        pl.semaphore_signal(barrier, inc=1, device_id=device_id, device_id_type=MESH)

    keys[0, core, 0:1, :] = cluster_ref[...].astype(jnp.float32)
    keys[0, core, 1:2, :] = rank_ref[...].astype(jnp.float32)

    def unit(r):
        wide = x_ref[pl.ds(r * PART, PART), :].astype(jnp.float32)
        scale = 1.0 / jnp.sqrt(jnp.sum(wide * wide, axis=1, keepdims=True) + 1e-06)
        rows[0, r, core] = (wide * scale).astype(jnp.bfloat16)

    unit(0)
    pl.semaphore_wait(barrier, len(neighbours) + 1)
    key_across(0).start()
    for r in range(CHUNKS):
        if r:
            unit(r)
        forward(first[r])
        across(0, r).start()

    row_best[...] = jnp.full_like(row_best, -1.0)
    col_best[...] = jnp.full_like(col_best, -1.0)

    def columns_of(n):
        for g in range(CHIP // 128):
            r, which = g // 2, g % 2
            for k in range(2):
                line = keys[n, which, k : k + 1, r * PART : (r + 1) * PART]
                columns[n, k, g * 128 : (g + 1) * 128, :] = jnp.broadcast_to(line, (128, 128)).T

    def take(n, r, follow):
        if r == 0:
            key_hop(n).wait_recv()
        hop(n, r).wait_recv()
        forward(follow)
        if r == 0:
            key_across(n).start()
        across(n, r).start()

    def cross(n, r):
        across(n, r).wait_recv()
        if r == 0:
            key_across(n).wait_recv()

    def back(n, which, target):
        return pltpu.make_async_remote_copy(
            src_ref=outbox.at[n, which], dst_ref=inbox.at[n, core], send_sem=back_send.at[n, which],
            recv_sem=back_arrive.at[n, core], device_id=target, device_id_type=MESH,
        )

    def back_wait(n, which):
        pltpu.make_async_remote_copy(
            src_ref=outbox.at[n, which], dst_ref=inbox.at[n, which], send_sem=back_send.at[n, which],
            recv_sem=back_arrive.at[n, which], device_id=sibling, device_id_type=MESH,
        ).wait_recv()

    def flush(n):
        for g in range(CHIP // 128):
            r, which = g // 2, g % 2
            best = jnp.max(col_best[n, :, g * 128 : (g + 1) * 128], axis=0, keepdims=True)
            if n in made:
                mine = row_best[n, g * 128 : (g + 1) * 128, :].T
                best = jnp.maximum(best, jnp.max(mine, axis=0, keepdims=True))
            outbox[n, which, r : r + 1, :] = best
        if n:
            for which in range(2):
                back(n, which, device(OFFSET[n], which)).start()
        else:
            back(0, other, sibling).start()

    def run(op):
        {"take": take, "cross": cross, "columns": columns_of, "flush": flush}[op[0]](*op[1:])

    bits = [jnp.int32(0), x // 2, y // 2, z // 2]

    def keep(lhs, top, rhs, col, base, score):
        lines = pl.ds(top, score.shape[0])
        cluster, rank = columns[lhs, 0, lines, :], columns[lhs, 1, lines, :]
        best = row_best[lhs, lines, :]
        for q in range(score.shape[1] // 128):
            line = pl.ds(pl.multiple_of(base // 2 + q // 2 * PART, PART), PART)
            cluster_j = keys[rhs, q % 2, 0:1, line]
            rank_j = keys[rhs, q % 2, 1:2, line]
            same = jnp.where(cluster == cluster_j, score[:, q * 128 : (q + 1) * 128], -1.0)
            later = rank > rank_j
            best = jnp.maximum(best, jnp.where(later, same, -1.0))
            back = jnp.max(jnp.where(later, -1.0, same).reshape(score.shape[0] // 8, 8, 128), axis=0)
            lanes = pl.ds(pl.multiple_of(base + q * 128, 128), 128)
            col_best[col, :, lanes] = jnp.maximum(col_best[col, :, lanes], back)
        row_best[lhs, lines, :] = best

    def product(lhs, rhs):
        return lax.dot_general(lhs, rhs, (((1,), (1,)), ((), ())), preferred_element_type=jnp.float32)

    def decode(code):
        fields = ((1, 16), (16, 16), (256, 4), (1024, 16), (16384, 4), (65536, 4))
        return (lax.rem(lax.div(code, jnp.int32(d)), jnp.int32(m)) for d, m in fields)

    def short(code):
        s, t1, r1, t2, r2, axis = decode(code)
        turn = sum((axis == k).astype(jnp.int32) * bits[k] for k in range(1, 4))
        lhs = s + turn * (t1 - s)
        todo = []
        for t, r in ((t1, r1), (t2, r2)):
            rhs, at = t + turn * (s - t), r + 2 * turn
            col = rhs + (s == t).astype(jnp.int32) * (SLOTS - rhs)
            score = product(rows[lhs].reshape(CHIP, WIDTH), rows[rhs, at].reshape(2 * PART, WIDTH))
            todo.append((rhs, col, pl.multiple_of(at * 2 * PART, 2 * PART), score))
        for rhs, col, base, score in todo:
            keep(lhs, 0, rhs, col, base, score)

    def half(code):
        s, t1, b1, t2, b2, a = decode(code)
        todo = []
        for t, b in ((t1, b1), (t2, b2)):
            score = product(
                rows[s, pl.ds(2 * a, 2)].reshape(ROWS, WIDTH), rows[t, pl.ds(2 * b, 2)].reshape(ROWS, WIDTH)
            )
            todo.append((t, pl.multiple_of(b * ROWS, ROWS), score))
        for t, base, score in todo:
            keep(s, pl.multiple_of(a * ROWS, ROWS), t, t, base, score)

    def long(code):
        s, t, *_ = decode(code)
        keep(s, 0, t, t, 0, product(rows[s].reshape(CHIP, WIDTH), rows[t].reshape(CHIP, WIDTH)))

    def encode(job):
        scale = (1, 16, 256, 1024, 16384, 65536)
        return sum(a * b for a, b in zip(job, scale))

    codes = []
    for _, _, jobs in steps:
        one, two = encode(jobs[0]), encode(jobs[1])
        codes.append(one + core * (two - one))

    def body(i, carry):
        code, wide = jnp.int32(0), jnp.int32(0)
        for k, (_, kind, _) in enumerate(steps):
            code = jnp.where(i == k, codes[k], code)
            if kind != "short":
                wide = jnp.where(i == k, ("short", "long", "half").index(kind), wide)
        for low in range(0, len(steps), GROUP):
            group = [(k, steps[k][0]) for k in range(low, min(low + GROUP, len(steps))) if steps[k][0]]

            @pl.when((i >= low) & (i < low + GROUP))
            def _(group=group):
                for k, ops in group:

                    @pl.when(i == k)
                    def _(ops=ops):
                        for op in ops:
                            run(op)

        @pl.when(wide == 0)
        def _():
            short(code)

        @pl.when(wide == 1)
        def _():
            long(code)

        @pl.when(wide == 2)
        def _():
            half(code)

        return carry

    for r in range(CHUNKS):
        cross(0, r)
    columns_of(0)
    lax.fori_loop(0, len(steps), body, 0)
    for op in rest:
        run(op)
    for n in range(SLOTS):
        for r in range(copies(n)):
            across(n, r).wait_send()
            if n:
                hop(n, r).wait_send()
        key_across(n).wait_send()
        if n:
            key_hop(n).wait_send()

    total = outbox[0, core]
    for n in range(1, SLOTS):
        for which in range(2):
            back_wait(n, which)
            total = jnp.maximum(total, inbox[n, which])
    back_wait(0, other)
    out_ref[...] = jnp.maximum(total, inbox[0, other])
    for n in range(1, SLOTS):
        for which in range(2):
            back(n, which, sibling).wait_send()
    back(0, other, sibling).wait_send()


def local(embeddings, cluster_ids, priority):
    steps, rest, made, _ = plan()
    first = sends(steps)
    dma = pltpu.SemaphoreType.DMA
    best = pl.pallas_call(
        functools.partial(kernel, first, steps, rest, made),
        out_shape=jax.ShapeDtypeStruct((CHUNKS, PART), jnp.float32),
        in_specs=[pl.BlockSpec(memory_space=pltpu.VMEM)] * 3,
        out_specs=pl.BlockSpec(memory_space=pltpu.VMEM),
        scratch_shapes=[
            pltpu.VMEM((SLOTS, CHUNKS, 2, PART, WIDTH), jnp.bfloat16),
            pltpu.VMEM((SLOTS, 2, 2, ROWS), jnp.float32),
            pltpu.VMEM((SLOTS, 2, CHIP, 128), jnp.float32),
            pltpu.VMEM((SLOTS, CHIP, 128), jnp.float32),
            pltpu.VMEM((SLOTS + 1, 8, CHIP), jnp.float32),
            pltpu.VMEM((SLOTS, 2, CHUNKS, PART), jnp.float32),
            pltpu.VMEM((SLOTS, 2, CHUNKS, PART), jnp.float32),
            dma((SLOTS, CHUNKS)),
            dma((SLOTS, CHUNKS)),
            dma((SLOTS, CHUNKS)),
            dma((SLOTS, CHUNKS)),
            dma((SLOTS,)),
            dma((SLOTS,)),
            dma((SLOTS,)),
            dma((SLOTS,)),
            dma((SLOTS, 2)),
            dma((SLOTS, 2)),
        ],
        compiler_params=pltpu.CompilerParams(
            collective_id=0, has_side_effects=True, vmem_limit_bytes=60 * 2**20
        ),
    )(embeddings, cluster_ids.reshape(1, ROWS), priority.reshape(1, ROWS))
    return best.reshape(ROWS)


def solution(mesh):
    placed = (P(("grp", "blk"), None), P(("grp", "blk"), None), P(("grp", "blk")))
    return jax.shard_map(
        local, mesh=mesh, in_specs=placed, out_specs=P(("grp", "blk")), check_vma=False
    )
```

time: 102 us -> 95.9 us (0.940)
  Pallas kernels: 101 us -> 94.4 us
    pallas_call x1, Pallas kernels: 101 us -> 94.4 us  [local(): pl.pallas_call(functools.partial(kernel, first, steps, rest, made), out_s...]
where the time goes in v3:
time: 95.9 us; the launch traced here: 95.7 us
  Pallas kernels  94.4 us (98%)
  local copies, waits for them, and re-layouts  1.26 us (1%)
    pallas_call x1, Pallas kernels, local(): pl.pallas_call(functools.partial(kernel, first, steps, rest, made), out_s...  94.4 us

profile of v3, /device:TPU:1, one launch (start us, length us, event | category | flops | bytes accessed | tf_op | source)
XLA Modules:
  0.0 95.7 jit_solution(10367601635594735241)
XLA Ops:
  0.0 94.4 %shard_map.37 = f32[4,128]{1,0:T(4,128)} custom-call(bf16[512,1024]{1,0:T(8,128)(2,1)} %x_ref.1, s32[1,512]{1,0:T(1,128)} %bitcast.4, s32[1,512]{1,0:T(1,128)} %bitcast.5), custom_call_target="tpu_custom_call" | custom-call | tf_op jit(solution)/shard_map/pallas_call | solution.py:522
  94.4 1.3 %copy.5 = f32[512]{0:T(512)} copy(f32[512]{0:T(512)} %bitcast.3) | data formatting | bytes 4096

commit v4 on v3

--- a/solution.py
+++ b/solution.py
@@ -46,11 +46,13 @@
 
 
 def covers(n, r):
-    return (2 * r, 2 * r + 1) if TREE[n][3] == 2 else (r,)
+    return (2 * r, 2 * r + 1) if copies(n) == 2 else (r,)
 
 
 def copies(n):
-    return 2 if TREE[n][3] == 2 else QUARTERS
+    second = [m for m in range(1, SLOTS) if TREE[m][3] == 2]
+    chained = TREE[n][1] in second or n in [TREE[m][1] for m in second]
+    return 2 if n in second and not chained else QUARTERS
 
 
 def first_on_link(m):
@@ -91,7 +93,15 @@
             if min(d, e) not in best or cost < best[min(d, e)][0]:
                 best[min(d, e)] = (cost, s, t, axis)
     assert len(best) == SIDE**3 // 2 + 3
-    return [b[1:] for b in sorted(best.values())]
+    pairs = [b[1:] for b in sorted(best.values())]
+    left = {0} | {n for s, t, axis in pairs if axis for n in (s, t)}
+    out = []
+    for s, t, axis in pairs:
+        if s not in left and t in left:
+            s, t = t, s
+        left.add(s)
+        out.append((s, t, axis))
+    return out
 
 
 def plan():
@@ -266,7 +276,7 @@
 
 def kernel(first, steps, rest, made, x_ref, cluster_ref, rank_ref, out_ref, rows, keys, columns, row_best, col_best, outbox,
            inbox, send, arrive, send_sib, arrive_sib, key_send, key_arrive, key_send_sib, key_arrive_sib,
-           back_send, back_arrive):
+           back_send, back_arrive, staged, stage):
     grp, z = lax.axis_index("grp"), lax.axis_index("blk")
     x, y, core = grp // (2 * SIDE), grp // 2 % SIDE, grp % 2
     other = 1 - core
@@ -319,6 +329,12 @@
             if r == 0:
                 key_hop(n).start()
 
+    def load(r):
+        part_r = pl.ds(r * PART, PART)
+        return pltpu.make_async_copy(x_ref.at[part_r], staged.at[part_r], stage.at[r])
+
+    for r in range(CHUNKS):
+        load(r).start()
     barrier = pltpu.get_barrier_semaphore()
     for device_id in neighbours + [sibling]:
         pl.semaphore_signal(barrier, inc=1, device_id=device_id, device_id_type=MESH)
@@ -327,10 +343,13 @@
     keys[0, core, 1:2, :] = rank_ref[...].astype(jnp.float32)
 
     def unit(r):
-        wide = x_ref[pl.ds(r * PART, PART), :].astype(jnp.float32)
+        load(r).wait()
+        wide = staged[pl.ds(r * PART, PART), :].astype(jnp.float32)
         scale = 1.0 / jnp.sqrt(jnp.sum(wide * wide, axis=1, keepdims=True) + 1e-06)
         rows[0, r, core] = (wide * scale).astype(jnp.bfloat16)
 
+    row_best[...] = jnp.full_like(row_best, -1.0)
+    col_best[...] = jnp.full_like(col_best, -1.0)
     unit(0)
     pl.semaphore_wait(barrier, len(neighbours) + 1)
     key_across(0).start()
@@ -340,8 +359,6 @@
         forward(first[r])
         across(0, r).start()
 
-    row_best[...] = jnp.full_like(row_best, -1.0)
-    col_best[...] = jnp.full_like(col_best, -1.0)
 
     def columns_of(n):
         for g in range(CHIP // 128):
@@ -522,7 +539,7 @@
     best = pl.pallas_call(
         functools.partial(kernel, first, steps, rest, made),
         out_shape=jax.ShapeDtypeStruct((CHUNKS, PART), jnp.float32),
-        in_specs=[pl.BlockSpec(memory_space=pltpu.VMEM)] * 3,
+        in_specs=[pl.BlockSpec(memory_space=pl.ANY)] + [pl.BlockSpec(memory_space=pltpu.VMEM)] * 2,
         out_specs=pl.BlockSpec(memory_space=pltpu.VMEM),
         scratch_shapes=[
             pltpu.VMEM((SLOTS, CHUNKS, 2, PART, WIDTH), jnp.bfloat16),
@@ -542,6 +559,8 @@
             dma((SLOTS,)),
             dma((SLOTS, 2)),
             dma((SLOTS, 2)),
+            pltpu.VMEM((ROWS, WIDTH), jnp.bfloat16),
+            dma((CHUNKS,)),
         ],
         compiler_params=pltpu.CompilerParams(
             collective_id=0, has_side_effects=True, vmem_limit_bytes=60 * 2**20

time: 95.9 us -> 94.9 us (0.990)
  Pallas kernels: 94.4 us -> 93.4 us
    pallas_call x1, Pallas kernels: 94.4 us -> 93.4 us  [local(): pl.pallas_call(functools.partial(kernel, first, steps, rest, made), out_s...]
where the time goes in v4:
time: 94.9 us; the launch traced here: 94.7 us
  Pallas kernels  93.4 us (98%)
  local copies, waits for them, and re-layouts  1.26 us (1%)
    pallas_call x1, Pallas kernels, local(): pl.pallas_call(functools.partial(kernel, first, steps, rest, made), out_s...  93.4 us

profile of v4, /device:TPU:1, one launch (start us, length us, event | category | flops | bytes accessed | tf_op | source)
XLA Modules:
  0.0 94.7 jit_solution(4649705651499086439)
XLA Ops:
  0.0 93.4 %shard_map.37 = f32[4,128]{1,0:T(4,128)} custom-call(bf16[512,1024]{1,0:T(8,128)(2,1)} %x_ref.1, s32[1,512]{1,0:T(1,128)} %bitcast.4, s32[1,512]{1,0:T(1,128)} %bitcast.5), custom_call_target="tpu_custom_call" | custom-call | tf_op jit(solution)/shard_map/pallas_call | solution.py:539
  93.4 1.3 %copy.5 = f32[512]{0:T(512)} copy(f32[512]{0:T(512)} %bitcast.3) | data formatting | bytes 4096

commit v5 on v4

--- a/solution.py
+++ b/solution.py
@@ -525,7 +525,8 @@
             back_wait(n, which)
             total = jnp.maximum(total, inbox[n, which])
     back_wait(0, other)
-    out_ref[...] = jnp.maximum(total, inbox[0, other])
+    out_ref[0] = total
+    out_ref[1] = inbox[0, other]
     for n in range(1, SLOTS):
         for which in range(2):
             back(n, which, sibling).wait_send()
@@ -538,7 +539,7 @@
     dma = pltpu.SemaphoreType.DMA
     best = pl.pallas_call(
         functools.partial(kernel, first, steps, rest, made),
-        out_shape=jax.ShapeDtypeStruct((CHUNKS, PART), jnp.float32),
+        out_shape=jax.ShapeDtypeStruct((2, CHUNKS, PART), jnp.float32),
         in_specs=[pl.BlockSpec(memory_space=pl.ANY)] + [pl.BlockSpec(memory_space=pltpu.VMEM)] * 2,
         out_specs=pl.BlockSpec(memory_space=pltpu.VMEM),
         scratch_shapes=[
@@ -566,7 +567,7 @@
             collective_id=0, has_side_effects=True, vmem_limit_bytes=60 * 2**20
         ),
     )(embeddings, cluster_ids.reshape(1, ROWS), priority.reshape(1, ROWS))
-    return best.reshape(ROWS)
+    return jnp.maximum(best[0], best[1]).reshape(ROWS)
 
 
 def solution(mesh):

time: 94.9 us -> 94.8 us (level)
  other arithmetic: 0 us -> 1.27 us
  local copies, waits for them, and re-layouts: 1.26 us -> 0 us
    max x0 -> x1, other arithmetic: none -> 1.27 us  [local(): return jnp.maximum(best[0], best[1]).reshape(ROWS)]
    unnamed x1 -> x0, local copies, waits for them, and re-layouts: 1.26 us -> none
where the time goes in v5:
time: 94.8 us; the launch traced here: 94.7 us
  Pallas kernels  93.4 us (99%)
  other arithmetic  1.27 us (1%)
    pallas_call x1, Pallas kernels, local(): pl.pallas_call(functools.partial(kernel, first, steps, rest, made), out_s...  93.4 us

profile of v5, /device:TPU:1, one launch (start us, length us, event | category | flops | bytes accessed | tf_op | source)
XLA Modules:
  0.0 94.7 jit_solution(13109362228126003799)
XLA Ops:
  0.0 93.4 %shard_map.37 = f32[2,4,128]{2,1,0:T(4,128)} custom-call(bf16[512,1024]{1,0:T(8,128)(2,1)} %x_ref.1, s32[1,512]{1,0:T(1,128)} %bitcast.4, s32[1,512]{1,0:T(1,128)} %bitcast.5), custom_call_target="tpu_custom_call" | custom-call | tf_op jit(solution)/shard_map/pallas_call | solution.py:540
  93.4 1.3 %maximum_bitcast_fusion = f32[512]{0:T(512)} fusion(f32[2,4,128]{2,1,0:T(4,128)} %shard_map.37), kind=kLoop, calls=%fused_computation | loop fusion | flops 512 | bytes 6144 | tf_op jit(solution)/shard_map/max | solution.py:570
